TPU v7x, 512 devices: a whole 4x4x16 slice. The times are simulated.
512 devices in a mesh: gx: 32 (over y, x, core), gy: 16 (over z).
Axes of the slice: x: 4, y: 4, z: 16, core: 2. Of those that a mesh axis runs over, the one named last changes fastest.
Arguments:
- basis: float32 [32, 256, 128, 256], P(None, 'gx', 'gy'), may hold values from -6 to 6
- rhs: float32 [256, 128, 256], P('gx', 'gy'), may hold values from -12 to 12
- extra_diag: float32 [256, 128, 256], P('gx', 'gy'), may hold values from 0.02 to 0.5
- coeff: float32 [3, 256, 128, 256], P(None, 'gx', 'gy'), may hold values from 0.3 to 3
Outputs:
- guess: float32 [256, 128, 256], P('gx', 'gy')
- stepped: float32 [256, 128, 256], P('gx', 'gy')
All inputs are finite; a program needn't handle non-finite values.
Results may differ from a plain program's by a relative error of at most 0.0003.
Values sent between devices are 32-bit elements; how exact they have to be, the bound alone decides.
A program may use at most 64 MiB of HBM per device.

v0:
```python
import jax
import jax.numpy as jnp
from jax import lax
from jax.sharding import PartitionSpec as P

precise = lax.Precision.HIGHEST


def shifted(block, axis, distance):
    devices = range(lax.axis_size(axis))
    route = [(i - distance, i) for i in devices if i - distance in devices]
    return lax.ppermute(block, axis, route)


def padded_2(cells, sides, width):
    for axis, dim in sides:
        count = lax.axis_size(axis)
        ends = count - 1
        head = lax.slice_in_dim(cells, 0, width, axis=dim)
        tail = lax.slice_in_dim(cells, cells.shape[dim] - width, cells.shape[dim], axis=dim)
        cells = jnp.concatenate(
            [
                lax.ppermute(tail, axis, [(i, (i + 1) % count) for i in range(ends)]),
                cells,
                lax.ppermute(head, axis, [((i + 1) % count, i) for i in range(ends)]),
            ],
            axis=dim,
        )
    return cells


def flux_apply(padded, coeff_pad, extra):
    center = padded[:, 1:-1, 1:-1]
    coeff_mid = coeff_pad[:, 1:-1, 1:-1]
    flux_x = coeff_mid[0] * (center - padded[:, 2:, 1:-1])
    flux_y = coeff_mid[1] * (center - padded[:, 1:-1, 2:])
    below_x = coeff_pad[0, :-2, 1:-1] * (padded[:, :-2, 1:-1] - center)
    below_y = coeff_pad[1, 1:-1, :-2] * (padded[:, 1:-1, :-2] - center)
    next_z = jnp.concatenate([center[..., 1:], jnp.zeros_like(center[..., :1])], axis=-1)
    flux_z = coeff_mid[2] * (center - next_z)
    below_z = jnp.concatenate([jnp.zeros_like(flux_z[..., :1]), flux_z[..., :-1]], axis=-1)
    return extra * center + flux_x + flux_y + flux_z - below_x - below_y - below_z


def small_solve(matrix, vector):
    lower = jnp.linalg.cholesky(matrix)
    middle = lax.linalg.triangular_solve(lower, vector[:, None], left_side=True, lower=True)
    result = lax.linalg.triangular_solve(
        lower, middle, left_side=True, lower=True, transpose_a=True
    )
    return result[:, 0]


def on_device(basis, rhs, extra_diag, coeff):
    lower_x = shifted(coeff[0][-1:], "gx", 1)
    lower_y = shifted(coeff[1][:, -1:], "gy", 1)
    coeff_pad = jnp.pad(coeff, ((0, 0), (1, 1), (1, 1), (0, 0)))
    coeff_pad = coeff_pad.at[0, 0, 1:-1].set(lower_x[0])
    coeff_pad = coeff_pad.at[1, 1:-1, 0].set(lower_y[:, 0])
    count = basis.shape[0]
    flat_basis = basis.reshape(count, -1)
    padded_basis = padded_2(basis, (("gx", 1), ("gy", 2)), 1)
    applied = flux_apply(padded_basis, coeff_pad, extra_diag)
    local_gram = jnp.dot(flat_basis, applied.reshape(count, -1).T, precision=precise)
    local_proj = jnp.dot(flat_basis, rhs.reshape(-1), precision=precise)
    gram, projected = lax.psum((local_gram, local_proj), ("gx", "gy"))
    gram = 0.5 * (gram + gram.T)
    weights = small_solve(gram, projected)
    guess = jnp.tensordot(weights, basis, axes=1, precision=precise)
    residual = rhs - jnp.tensordot(weights, applied, axes=1, precision=precise)
    coeff_mid = coeff_pad[:, 1:-1, 1:-1]
    below_kz = jnp.concatenate([jnp.zeros_like(coeff[2][..., :1]), coeff[2][..., :-1]], axis=-1)
    diagonal = (
        extra_diag
        + coeff_mid[0]
        + coeff_mid[1]
        + coeff_mid[2]
        + coeff_pad[0, :-2, 1:-1]
        + coeff_pad[1, 1:-1, :-2]
        + below_kz
    )
    direction = residual / diagonal
    direction_pad = padded_2(direction, (("gx", 0), ("gy", 1)), 1)
    applied_dir = flux_apply(direction_pad[None], coeff_pad, extra_diag)[0]
    local_corr = jnp.dot(flat_basis, applied_dir.reshape(-1), precision=precise)
    correction = lax.psum(local_corr, ("gx", "gy"))
    shift_coef = small_solve(gram, correction)
    update = direction - jnp.tensordot(shift_coef, basis, axes=1, precision=precise)
    update_pad = padded_2(update, (("gx", 0), ("gy", 1)), 1)
    applied_upd = flux_apply(update_pad[None], coeff_pad, extra_diag)[0]
    numerator, denominator = lax.psum(
        (jnp.sum(residual * update), jnp.sum(update * applied_upd)), ("gx", "gy")
    )
    step_size = numerator / denominator
    return (guess, guess + step_size * update)


def solution(mesh):
    placed = (
        P(None, "gx", "gy", None),
        P("gx", "gy", None),
        P("gx", "gy", None),
        P(None, "gx", "gy", None),
    )
    return jax.shard_map(
        on_device,
        mesh=mesh,
        in_specs=placed,
        out_specs=(P("gx", "gy", None), P("gx", "gy", None)),
        check_vma=False,
    )
```

profile of v0, /device:TPU:1, one launch (start us, length us, event | category | flops | bytes accessed | tf_op | source)
XLA Modules:
  0.0 410.9 jit_solution(2487708091433647536)
XLA Ops:
  0.6 0.7 slice_bitcast_fusion.7
  1.3 4.6 %collective-permute-start = (f32[1,8,256]{2,1,0:T(8,128)S(1)}, f32[1,8,256]{2,1,0:T(8,128)S(1)}, u32[]{:S(2)}, u32[]{:S(2)}) collective-permute-start(f32[1,8,256]{2,1,0:T(8,128)S(1)} %slice_bitcast_fusion.7), channel_id=1, source_target_pairs={{0,16},{16,32},{32,48},{48,64},{64,80},{80,96},{96,112},{112,128},... | collective-permute-start | bytes 24584 | tf_op jit(solution)/shard_map/ppermute | solution.py:12
  6.0 2.8 copy.11
  8.8 0.9 fusion.53
  9.7 1.9 collective-permute-start.3
  11.6 3.5 collective-permute-start.1
  15.2 2.8 collective-permute-start.2
  18.0 1.9 slice.287
  20.0 0.2 scatter.6
  20.3 3.0 subtract_multiply_fusion
  23.5 1.4 collective-permute-start.4
  24.9 4.2 %collective-permute-start.5 = (f32[32,10,1,256]{3,0,2,1:T(8,128)S(1)}, f32[32,10,1,256]{3,0,2,1:T(8,128)S(1)}, u32[]{:S(2)}, u32[]{:S(2)}) collective-permute-start(f32[32,10,1,256]{3,0,2,1:T(8,128)S(1)} %get-tuple-element.38), channel_id=1, source_target_pairs={{0,1},{1,2},{2,3},{3,4},{4,5},{5,6},{6,7},{7,8},{8,9},{9,10},{10,1... | collective-permute-start | bytes 983048 | tf_op jit(solution)/shard_map/ppermute | solution.py:23
  29.1 2.8 convolution_bitcast_fusion.6
  31.9 2.9 collective-permute-done.4
  34.8 1.8 collective-permute-done.5
  36.6 2.9 fusion.3
  39.5 1.3 copy-done.3
  40.8 2.9 convolution_bitcast_fusion
  43.7 110.2 %all-reduce.9 = (f32[32,1]{0,1:T(1,128)S(1)}, f32[32,32]{1,0:T(8,128)S(1)}) all-reduce(f32[32,1]{0,1:T(1,128)S(1)} %convolution_bitcast_fusion.6, f32[32,32]{1,0:T(8,128)S(1)} %convolution_bitcast_fusion), channel_id=1, replica_groups=mesh['gx'=32,'gy'=16] {'gx','gy'}, use_global_device_ids=true, to_apply=%region_3.0 | all-reduce | flops 1056 | bytes 8448 | tf_op jit(solution)/shard_map/psum | solution.py:66
  154.1 2.9 cholesky.18
  157.1 0.6 compare_reduce_fusion
  157.7 0.7 fusion.39
  158.4 2.4 custom-call.11
  160.8 0.2 convolution_bitcast_fusion.4
  160.9 0.1 convolution_bitcast_fusion.3
  161.1 2.7 fusion.56
  163.9 3.1 collective-permute-start.6
  167.0 1.9 collective-permute-start.7
  168.9 3.0 collective-permute-done.7
  172.0 3.6 collective-permute-start.8
  175.6 1.3 collective-permute-start.9
  176.9 1.2 copy.38
  178.2 1.9 collective-permute-done.9
  180.4 1.7 convolution_bitcast_fusion.5
  182.1 103.9 %psum.37 = f32[32,1]{0,1:T(1,128)S(1)} all-reduce(f32[32,1]{0,1:T(1,128)S(1)} %convolution_bitcast_fusion.5), channel_id=1, replica_groups=mesh['gx'=32,'gy'=16] {'gx','gy'}, use_global_device_ids=true, to_apply=%region_4.8 | all-reduce | flops 32 | bytes 256 | tf_op jit(solution)/shard_map/psum | solution.py:86
  286.0 0.1 convolution_bitcast_fusion.2
  286.1 0.1 convolution_bitcast_fusion.1
  286.3 2.2 fusion.47
  288.5 3.7 collective-permute-start.10
  292.2 1.9 collective-permute-start.11
  294.1 3.0 collective-permute-done.11
  297.2 1.3 collective-permute-start.12
  298.5 1.5 collective-permute-start.13
  300.0 2.2 fusion.49
  302.3 0.7 collective-permute-done.13
  303.1 0.7 fusion.19
  303.8 105.1 %all-reduce.8 = (f32[]{:T(128)}, f32[]{:T(128)}) all-reduce(f32[]{:T(128)} %get-tuple-element.30, f32[]{:T(128)} %get-tuple-element.29), channel_id=1, replica_groups=mesh['gx'=32,'gy'=16] {'gx','gy'}, use_global_device_ids=true, to_apply=%region_6.10 | all-reduce | flops 2 | bytes 16 | tf_op jit(solution)/shard_map/psum | solution.py:91
  410.2 0.7 multiply_add_fusion
  (48 shorter events, 1.1 us)
Async XLA Ops:
  1.3 10.2 %copy-start.6 = (f32[3,8,8,256]{3,2,1,0:T(8,128)S(1)}, f32[3,8,8,256]{3,2,1,0:T(8,128)}, u32[]{:S(2)}) copy-start(f32[3,8,8,256]{3,2,1,0:T(8,128)} %param.16) | copy-start | bytes 589828
  1.3 18.7 %collective-permute-start = (f32[1,8,256]{2,1,0:T(8,128)S(1)}, f32[1,8,256]{2,1,0:T(8,128)S(1)}, u32[]{:S(2)}, u32[]{:S(2)}) collective-permute-start(f32[1,8,256]{2,1,0:T(8,128)S(1)} %slice_bitcast_fusion.7), channel_id=1, source_target_pairs={{0,16},{16,32},{32,48},{48,64},{64,80},{80,96},{96,112},{112,128},... | collective-permute-start | bytes 24584 | tf_op jit(solution)/shard_map/ppermute | solution.py:12
  8.8 11.2 %copy-start.1 = (f32[32,8,8,256]{3,0,2,1:T(8,128)}, f32[32,8,8,256]{3,0,2,1:T(8,128)S(1)}, u32[]{:S(2)}) copy-start(f32[32,8,8,256]{3,0,2,1:T(8,128)S(1)} %copy.11) | copy-start | bytes 6291460
  9.7 10.6 %collective-permute-start.3 = (f32[32,1,8,256]{3,0,2,1:T(8,128)}, f32[32,1,8,256]{3,0,2,1:T(8,128)S(1)}, u32[]{:S(2)}, u32[]{:S(2)}) collective-permute-start(f32[32,1,8,256]{3,0,2,1:T(8,128)} %get-tuple-element.42), channel_id=1, source_target_pairs={{0,16},{16,32},{32,48},{48,64},{64,80},{80,96},{96,112},{112,128},... | collective-permute-start | bytes 786440 | tf_op jit(solution)/shard_map/ppermute | solution.py:23
  11.6 8.5 %collective-permute-start.1 = (f32[8,1,256]{2,1,0:T(1,128)S(1)}, f32[8,1,256]{2,1,0:T(1,128)S(1)}, u32[]{:S(2)}, u32[]{:S(2)}) collective-permute-start(f32[8,1,256]{2,1,0:T(1,128)S(1)} %slice.280), channel_id=1, source_target_pairs={{0,1},{1,2},{2,3},{3,4},{4,5},{5,6},{6,7},{7,8},{8,9},{9,10},{10,1... | collective-permute-start | bytes 24584 | tf_op jit(solution)/shard_map/ppermute | solution.py:12
  15.2 5.1 %copy-start = (f32[32,8,8,256]{3,2,1,0:T(8,128)S(1)}, f32[32,8,8,256]{3,2,1,0:T(8,128)}, u32[]{:S(2)}) copy-start(f32[32,8,8,256]{3,2,1,0:T(8,128)} %param.13) | copy-start | bytes 6291460
  15.2 8.2 %collective-permute-start.2 = (f32[32,1,8,256]{3,0,2,1:T(8,128)}, f32[32,1,8,256]{3,0,2,1:T(8,128)S(1)}, u32[]{:S(2)}, u32[]{:S(2)}) collective-permute-start(f32[32,1,8,256]{3,0,2,1:T(8,128)} %get-tuple-element.41), channel_id=1, source_target_pairs={{16,0},{32,16},{48,32},{64,48},{80,64},{96,80},{112,96},{128,112},... | collective-permute-start | bytes 786440 | tf_op jit(solution)/shard_map/ppermute | solution.py:25
  20.3 8.8 %copy-start.5 = (f32[8,8,256]{2,1,0:T(8,128)S(1)}, f32[8,8,256]{2,1,0:T(8,128)}, u32[]{:S(2)}) copy-start(f32[8,8,256]{2,1,0:T(8,128)} %param.14) | copy-start | bytes 196612
  23.4 13.2 %copy-start.2 = (f32[32,8,8,256]{3,0,2,1:T(8,128)S(1)}, f32[32,8,8,256]{3,0,2,1:T(8,128)}, u32[]{:S(2)}) copy-start(f32[32,8,8,256]{3,0,2,1:T(8,128)} %copy-done.1) | copy-start | bytes 6291460
  23.4 13.2 %copy-start.4 = (f32[8,8,256]{2,1,0:T(8,128)S(1)}, f32[8,8,256]{2,1,0:T(8,128)}, u32[]{:S(2)}) copy-start(f32[8,8,256]{2,1,0:T(8,128)} %param.15) | copy-start | bytes 196612
  23.5 11.3 %collective-permute-start.4 = (f32[32,10,1,256]{3,0,2,1:T(8,128)S(1)}, f32[32,10,1,256]{3,0,2,1:T(8,128)S(1)}, u32[]{:S(2)}, u32[]{:S(2)}) collective-permute-start(f32[32,10,1,256]{3,0,2,1:T(8,128)S(1)} %get-tuple-element.37), channel_id=1, source_target_pairs={{1,0},{2,1},{3,2},{4,3},{5,4},{6,5},{7,6},{8,7},{9,8},{10,9},{11,1... | collective-permute-start | bytes 983048 | tf_op jit(solution)/shard_map/ppermute | solution.py:25
  24.9 11.7 %collective-permute-start.5 = (f32[32,10,1,256]{3,0,2,1:T(8,128)S(1)}, f32[32,10,1,256]{3,0,2,1:T(8,128)S(1)}, u32[]{:S(2)}, u32[]{:S(2)}) collective-permute-start(f32[32,10,1,256]{3,0,2,1:T(8,128)S(1)} %get-tuple-element.38), channel_id=1, source_target_pairs={{0,1},{1,2},{2,3},{3,4},{4,5},{5,6},{6,7},{7,8},{8,9},{9,10},{10,1... | collective-permute-start | bytes 983048 | tf_op jit(solution)/shard_map/ppermute | solution.py:23
  39.5 1.3 copy-start.3
  163.9 5.0 %collective-permute-start.6 = (f32[1,8,256]{2,1,0:T(8,128)S(1)}, f32[1,8,256]{2,1,0:T(8,128)S(1)}, u32[]{:S(2)}, u32[]{:S(2)}) collective-permute-start(f32[1,8,256]{2,1,0:T(8,128)S(1)} %get-tuple-element.56), channel_id=1, source_target_pairs={{0,16},{16,32},{32,48},{48,64},{64,80},{80,96},{96,112},{112,128},... | collective-permute-start | bytes 24584 | tf_op jit(solution)/shard_map/ppermute | solution.py:23
  167.0 5.0 %collective-permute-start.7 = (f32[1,8,256]{2,1,0:T(8,128)S(1)}, f32[1,8,256]{2,1,0:T(8,128)S(1)}, u32[]{:S(2)}, u32[]{:S(2)}) collective-permute-start(f32[1,8,256]{2,1,0:T(8,128)S(1)} %get-tuple-element.57), channel_id=1, source_target_pairs={{16,0},{32,16},{48,32},{64,48},{80,64},{96,80},{112,96},{128,112},... | collective-permute-start | bytes 24584 | tf_op jit(solution)/shard_map/ppermute | solution.py:25
  172.0 6.2 %collective-permute-start.8 = (f32[10,1,256]{2,1,0:T(1,128)S(1)}, f32[10,1,256]{2,1,0:T(1,128)S(1)}, u32[]{:S(2)}, u32[]{:S(2)}) collective-permute-start(f32[10,1,256]{2,1,0:T(1,128)S(1)} %get-tuple-element.52), channel_id=1, source_target_pairs={{0,1},{1,2},{2,3},{3,4},{4,5},{5,6},{6,7},{7,8},{8,9},{9,10},{10,1... | collective-permute-start | bytes 30728 | tf_op jit(solution)/shard_map/ppermute | solution.py:23
  175.6 4.4 %collective-permute-start.9 = (f32[10,1,256]{2,1,0:T(1,128)S(1)}, f32[10,1,256]{2,1,0:T(1,128)S(1)}, u32[]{:S(2)}, u32[]{:S(2)}) collective-permute-start(f32[10,1,256]{2,1,0:T(1,128)S(1)} %get-tuple-element.53), channel_id=1, source_target_pairs={{1,0},{2,1},{3,2},{4,3},{5,4},{6,5},{7,6},{8,7},{9,8},{10,9},{11,1... | collective-permute-start | bytes 30728 | tf_op jit(solution)/shard_map/ppermute | solution.py:25
  288.5 5.6 %collective-permute-start.10 = (f32[1,8,256]{2,1,0:T(8,128)S(1)}, f32[1,8,256]{2,1,0:T(8,128)S(1)}, u32[]{:S(2)}, u32[]{:S(2)}) collective-permute-start(f32[1,8,256]{2,1,0:T(8,128)S(1)} %get-tuple-element.54), channel_id=1, source_target_pairs={{0,16},{16,32},{32,48},{48,64},{64,80},{80,96},{96,112},{112,128},... | collective-permute-start | bytes 24584 | tf_op jit(solution)/shard_map/ppermute | solution.py:23
  292.2 5.0 %collective-permute-start.11 = (f32[1,8,256]{2,1,0:T(8,128)S(1)}, f32[1,8,256]{2,1,0:T(8,128)S(1)}, u32[]{:S(2)}, u32[]{:S(2)}) collective-permute-start(f32[1,8,256]{2,1,0:T(8,128)S(1)} %get-tuple-element.55), channel_id=1, source_target_pairs={{16,0},{32,16},{48,32},{64,48},{80,64},{96,80},{112,96},{128,112},... | collective-permute-start | bytes 24584 | tf_op jit(solution)/shard_map/ppermute | solution.py:25
  297.2 5.1 %collective-permute-start.12 = (f32[10,1,256]{2,1,0:T(1,128)S(1)}, f32[10,1,256]{2,1,0:T(1,128)S(1)}, u32[]{:S(2)}, u32[]{:S(2)}) collective-permute-start(f32[10,1,256]{2,1,0:T(1,128)S(1)} %get-tuple-element.50), channel_id=1, source_target_pairs={{0,1},{1,2},{2,3},{3,4},{4,5},{5,6},{6,7},{7,8},{8,9},{9,10},{10,1... | collective-permute-start | bytes 30728 | tf_op jit(solution)/shard_map/ppermute | solution.py:23
  298.5 4.4 %collective-permute-start.13 = (f32[10,1,256]{2,1,0:T(1,128)S(1)}, f32[10,1,256]{2,1,0:T(1,128)S(1)}, u32[]{:S(2)}, u32[]{:S(2)}) collective-permute-start(f32[10,1,256]{2,1,0:T(1,128)S(1)} %get-tuple-element.51), channel_id=1, source_target_pairs={{1,0},{2,1},{3,2},{4,3},{5,4},{6,5},{7,6},{8,7},{9,8},{10,9},{11,1... | collective-permute-start | bytes 30728 | tf_op jit(solution)/shard_map/ppermute | solution.py:25
where the time goes:
time: 412 us; the launch traced here: 411 us
  blocking collectives  319 us (77%)
  starting transfers between devices  36.8 us (9%)
  matrix products  15.1 us (4%)
  other arithmetic  14.3 us (3%)
  waiting for transfers between devices  13.3 us (3%)
  local copies, waits for them, and re-layouts  9.65 us (2%)
    psum x1, blocking collectives, on_device(): gram, projected = lax.psum((local_gram, local_proj), ('gx', 'gy'))  110 us
    psum x1, blocking collectives, on_device(): lax.psum((jnp.sum(residual * update), jnp.sum(update * applied_upd)), ('g...  105 us
    psum x1, blocking collectives, on_device(): correction = lax.psum(local_corr, ('gx', 'gy'))  104 us
    ppermute x6, starting transfers between devices, padded_2(): lax.ppermute(tail, axis, [(i, (i + 1) % count) for i in range(ends)])  17.8 us
    ppermute x6, waiting for transfers between devices, padded_2(): lax.ppermute(head, axis, [((i + 1) % count, i) for i in range(ends)])  11.5 us
    ppermute x6, starting transfers between devices, padded_2(): lax.ppermute(head, axis, [((i + 1) % count, i) for i in range(ends)])  10.9 us
  transfers between devices with their start and end apart: 14, of which 6 were waited for; matrix products, arithmetic and copies ran while one was open for 4% of the time, Pallas kernels for 0%

commit v1 on v0

--- a/solution.py
+++ b/solution.py
@@ -83,7 +83,7 @@
     direction_pad = padded_2(direction, (("gx", 0), ("gy", 1)), 1)
     applied_dir = flux_apply(direction_pad[None], coeff_pad, extra_diag)[0]
     local_corr = jnp.dot(flat_basis, applied_dir.reshape(-1), precision=precise)
-    correction = lax.psum(local_corr, ("gx", "gy"))
+    correction = jnp.sum(lax.all_gather(local_corr, ("gx", "gy")), axis=0)
     shift_coef = small_solve(gram, correction)
     update = direction - jnp.tensordot(shift_coef, basis, axes=1, precision=precise)
     update_pad = padded_2(update, (("gx", 0), ("gy", 1)), 1)

time: 412 us -> 764 us (1.85)
  waiting for transfers between devices: 13.3 us -> 453 us
  blocking collectives: 319 us -> 213 us
  between operations: 2.43 us -> 15.8 us
    unnamed x0 -> x2, waiting for transfers between devices: none -> 441 us
    psum x1 -> x0, blocking collectives: 104 us -> none  [on_device(): correction = lax.psum(local_corr, ('gx', 'gy'))]
  transfers between devices with their start and end apart: 14 -> 15, of which waited for: 6 -> 7; matrix products, arithmetic and copies ran while one was open for 4% -> 2% of each run, Pallas kernels for 0% -> 0%
where the time goes in v1:
time: 764 us; the launch traced here: 763 us
  waiting for transfers between devices  453 us (59%)
  blocking collectives  213 us (28%)
  starting transfers between devices  36.7 us (5%)
  matrix products  16.7 us (2%)
  between operations  15.8 us (2%)
  other arithmetic  14.4 us (2%)
  local copies, waits for them, and re-layouts  12.9 us (2%)
    unnamed x2, waiting for transfers between devices  441 us
    psum x1, blocking collectives, on_device(): gram, projected = lax.psum((local_gram, local_proj), ('gx', 'gy'))  110 us
    psum x1, blocking collectives, on_device(): lax.psum((jnp.sum(residual * update), jnp.sum(update * applied_upd)), ('g...  103 us
    ppermute x6, starting transfers between devices, padded_2(): lax.ppermute(tail, axis, [(i, (i + 1) % count) for i in range(ends)])  17.9 us
  transfers between devices with their start and end apart: 15, of which 7 were waited for; matrix products, arithmetic and copies ran while one was open for 2% of the time, Pallas kernels for 0%

profile of v1, /device:TPU:1, one launch (start us, length us, event | category | flops | bytes accessed | tf_op | source)
XLA Modules:
  0.0 762.9 jit_solution(17456044288111859184)
XLA Ops:
  7.2 0.7 slice_bitcast_fusion.7
  7.9 4.6 collective-permute-start
  12.5 2.8 copy.16
  15.4 0.9 fusion.54
  16.3 1.9 collective-permute-start.3
  18.2 3.5 collective-permute-start.1
  21.8 2.8 collective-permute-start.2
  24.6 1.9 slice.287
  26.6 0.2 scatter.6
  26.9 3.0 subtract_multiply_fusion
  30.1 1.4 collective-permute-start.4
  31.5 4.2 collective-permute-start.5
  35.7 2.8 convolution_bitcast_fusion.6
  38.5 2.9 collective-permute-done.4
  41.4 1.8 collective-permute-done.5
  43.2 2.9 fusion.3
  46.1 1.3 copy-done.3
  47.5 2.9 convolution_bitcast_fusion
  50.4 110.2 %all-reduce.10 = (f32[32,1]{0,1:T(1,128)S(1)}, f32[32,32]{1,0:T(8,128)S(1)}) all-reduce(f32[32,1]{0,1:T(1,128)S(1)} %convolution_bitcast_fusion.6, f32[32,32]{1,0:T(8,128)S(1)} %convolution_bitcast_fusion), channel_id=1, replica_groups=mesh['gx'=32,'gy'=16] {'gx','gy'}, use_global_device_ids=true, to_apply=%region_3.0 | all-reduce | flops 1056 | bytes 8448 | tf_op jit(solution)/shard_map/psum | solution.py:66
  160.7 2.9 cholesky.18
  163.7 0.6 compare_reduce_fusion
  164.3 0.7 fusion.39
  165.0 2.4 custom-call.11
  167.4 0.2 convolution_bitcast_fusion.4
  167.7 2.7 fusion.57
  170.5 3.1 collective-permute-start.6
  173.6 1.9 collective-permute-start.7
  175.6 3.0 collective-permute-done.7
  178.6 3.6 collective-permute-start.8
  182.3 1.3 collective-permute-start.9
  183.6 2.6 copy.43
  186.1 0.5 collective-permute-done.9
  187.0 3.3 convolution_bitcast_fusion.5
  190.3 0.3 dynamic-update-slice.8
  190.6 0.6 copy-done.7
  191.3 441.0 %all-reduce.13.cloned.1.call-done = f32[16384]{0:T(1024)} async-done(((f32[16384]{0:T(1024)}), f32[16384]{0:T(1024)}) %all-reduce.13.cloned.1.call-update) | async-done | bytes 65552
  632.2 0.9 reshape.130
  633.5 2.2 fusion.48
  635.8 3.2 collective-permute-start.10
  639.0 1.9 collective-permute-start.11
  641.0 3.0 collective-permute-done.11
  644.0 1.9 collective-permute-start.12
  645.9 1.3 collective-permute-start.13
  647.2 2.2 fusion.50
  649.4 0.9 collective-permute-done.13
  650.5 0.7 fusion.19
  651.2 102.9 %all-reduce.9 = (f32[]{:T(128)}, f32[]{:T(128)}) all-reduce(f32[]{:T(128)} %get-tuple-element.30, f32[]{:T(128)} %get-tuple-element.29), channel_id=1, replica_groups=mesh['gx'=32,'gy'=16] {'gx','gy'}, use_global_device_ids=true, to_apply=%region_6.10 | all-reduce | flops 2 | bytes 16 | tf_op jit(solution)/shard_map/psum | solution.py:91
  755.4 0.7 multiply_add_fusion
  (56 shorter events, 1.6 us)
Async XLA Ops:
  7.2 625.1 %all-reduce.13.cloned.1.call-start = ((), (), s32[]{:S(2)}) async-start(), calls=%async_computation | async-start | bytes 131072
  7.9 10.3 %copy-start.6 = (f32[3,8,8,256]{3,2,1,0:T(8,128)S(1)}, f32[3,8,8,256]{3,2,1,0:T(8,128)}, u32[]{:S(2)}) copy-start(f32[3,8,8,256]{3,2,1,0:T(8,128)} %param.16) | copy-start | bytes 589828
  7.9 18.7 %collective-permute-start = (f32[1,8,256]{2,1,0:T(8,128)S(1)}, f32[1,8,256]{2,1,0:T(8,128)S(1)}, u32[]{:S(2)}, u32[]{:S(2)}) collective-permute-start(f32[1,8,256]{2,1,0:T(8,128)S(1)} %slice_bitcast_fusion.7), channel_id=1, source_target_pairs={{0,16},{16,32},{32,48},{48,64},{64,80},{80,96},{96,112},{112,128},... | collective-permute-start | bytes 24584 | tf_op jit(solution)/shard_map/ppermute | solution.py:12
  15.4 11.2 %copy-start.1 = (f32[32,8,8,256]{3,0,2,1:T(8,128)}, f32[32,8,8,256]{3,0,2,1:T(8,128)S(1)}, u32[]{:S(2)}) copy-start(f32[32,8,8,256]{3,0,2,1:T(8,128)S(1)} %copy.16) | copy-start | bytes 6291460
  16.3 10.6 %collective-permute-start.3 = (f32[32,1,8,256]{3,0,2,1:T(8,128)}, f32[32,1,8,256]{3,0,2,1:T(8,128)S(1)}, u32[]{:S(2)}, u32[]{:S(2)}) collective-permute-start(f32[32,1,8,256]{3,0,2,1:T(8,128)} %get-tuple-element.42), channel_id=1, source_target_pairs={{0,16},{16,32},{32,48},{48,64},{64,80},{80,96},{96,112},{112,128},... | collective-permute-start | bytes 786440 | tf_op jit(solution)/shard_map/ppermute | solution.py:23
  18.2 8.6 %collective-permute-start.1 = (f32[8,1,256]{2,1,0:T(1,128)S(1)}, f32[8,1,256]{2,1,0:T(1,128)S(1)}, u32[]{:S(2)}, u32[]{:S(2)}) collective-permute-start(f32[8,1,256]{2,1,0:T(1,128)S(1)} %slice.280), channel_id=1, source_target_pairs={{0,1},{1,2},{2,3},{3,4},{4,5},{5,6},{6,7},{7,8},{8,9},{9,10},{10,1... | collective-permute-start | bytes 24584 | tf_op jit(solution)/shard_map/ppermute | solution.py:12
  21.8 5.2 copy-start
  21.8 8.2 %collective-permute-start.2 = (f32[32,1,8,256]{3,0,2,1:T(8,128)}, f32[32,1,8,256]{3,0,2,1:T(8,128)S(1)}, u32[]{:S(2)}, u32[]{:S(2)}) collective-permute-start(f32[32,1,8,256]{3,0,2,1:T(8,128)} %get-tuple-element.41), channel_id=1, source_target_pairs={{16,0},{32,16},{48,32},{64,48},{80,64},{96,80},{112,96},{128,112},... | collective-permute-start | bytes 786440 | tf_op jit(solution)/shard_map/ppermute | solution.py:25
  26.9 8.8 %copy-start.5 = (f32[8,8,256]{2,1,0:T(8,128)S(1)}, f32[8,8,256]{2,1,0:T(8,128)}, u32[]{:S(2)}) copy-start(f32[8,8,256]{2,1,0:T(8,128)} %param.14) | copy-start | bytes 196612
  30.0 13.2 %copy-start.2 = (f32[32,8,8,256]{3,0,2,1:T(8,128)S(1)}, f32[32,8,8,256]{3,0,2,1:T(8,128)}, u32[]{:S(2)}) copy-start(f32[32,8,8,256]{3,0,2,1:T(8,128)} %copy-done.1) | copy-start | bytes 6291460
  30.0 13.2 %copy-start.4 = (f32[8,8,256]{2,1,0:T(8,128)S(1)}, f32[8,8,256]{2,1,0:T(8,128)}, u32[]{:S(2)}) copy-start(f32[8,8,256]{2,1,0:T(8,128)} %param.15) | copy-start | bytes 196612
  30.1 11.3 %collective-permute-start.4 = (f32[32,10,1,256]{3,0,2,1:T(8,128)S(1)}, f32[32,10,1,256]{3,0,2,1:T(8,128)S(1)}, u32[]{:S(2)}, u32[]{:S(2)}) collective-permute-start(f32[32,10,1,256]{3,0,2,1:T(8,128)S(1)} %get-tuple-element.37), channel_id=1, source_target_pairs={{1,0},{2,1},{3,2},{4,3},{5,4},{6,5},{7,6},{8,7},{9,8},{10,9},{11,1... | collective-permute-start | bytes 983048 | tf_op jit(solution)/shard_map/ppermute | solution.py:25
  31.5 11.7 %collective-permute-start.5 = (f32[32,10,1,256]{3,0,2,1:T(8,128)S(1)}, f32[32,10,1,256]{3,0,2,1:T(8,128)S(1)}, u32[]{:S(2)}, u32[]{:S(2)}) collective-permute-start(f32[32,10,1,256]{3,0,2,1:T(8,128)S(1)} %get-tuple-element.38), channel_id=1, source_target_pairs={{0,1},{1,2},{2,3},{3,4},{4,5},{5,6},{6,7},{7,8},{8,9},{9,10},{10,1... | collective-permute-start | bytes 983048 | tf_op jit(solution)/shard_map/ppermute | solution.py:23
  46.1 1.3 copy-start.3
  170.5 5.0 collective-permute-start.6
  173.6 5.0 collective-permute-start.7
  178.6 7.5 collective-permute-start.8
  182.3 4.4 collective-permute-start.9
  190.6 0.6 copy-start.7
  635.8 5.1 collective-permute-start.10
  639.0 5.0 collective-permute-start.11
  644.0 5.4 collective-permute-start.12
  645.9 4.4 collective-permute-start.13
Sparse Core Ops, SparseCore 0:
  191.4 440.7 all-reduce.12
